TPU v7x, 128 devices: a whole 4x4x4 slice. The times are simulated.
128 devices in a mesh: fsdp: 16 (over x, z), tp: 8 (over y, core).
Axes of the slice: x: 4, y: 4, z: 4, core: 2. Of those that a mesh axis runs over, the one named last changes fastest.
Arguments:
- old_master: float32 [256, 4300, 128], P(('fsdp', 'tp')), may hold values from -0.046875 to 0.046875
- old_momentum: float32 [256, 4300, 128], P(('fsdp', 'tp')), may hold values from -6 to 6
- old_variance: float32 [256, 4300, 128], P(('fsdp', 'tp')), may hold values from 0.1 to 2
- flat_offsets: int32 [257], replicated, may hold values from 0 to 917504, as said below
- hidden_acts: bfloat16 [2048, 14336], P('fsdp', 'tp'), may hold values from -6 to 6
- out_grad: bfloat16 [2048, 8192], P('tp', 'fsdp'), may hold values from -0.29882812 to 0.29882812
Outputs:
- output: bfloat16 [2048, 8192], P('tp', 'fsdp')
- new_master: float32 [14336, 8192], P('tp', 'fsdp')
- new_momentum: float32 [14336, 8192], P('tp', 'fsdp')
- new_variance: float32 [14336, 8192], P('tp', 'fsdp')
Inputs may be any that keep to these rules, and one draw needn't show every extreme that they name: flat_offsets rises from 0 to 917504; entry k lies within 358 of k * 3584, and differs from it where k is a multiple of 32 strictly between 0 and 256; each piece holds between 2868 and 4300 granules, the largest reached by some piece in every draw; entries of a piece past its length are not part of the slab.
All inputs are finite; a program needn't handle non-finite values.
Results may differ from a plain program's by a relative error of at most 0.013.
Values may be sent and summed in bfloat16 or wider, within the bound.
No kernel may reach another device: no remote copies, remote signals or barrier semaphores. Data moves between devices by JAX's collectives and lax.ppermute only.
A program may use at most 192 MiB of HBM per device.

v0:
```python
import jax
import jax.numpy as jnp
from jax import lax
from jax.sharding import PartitionSpec as P

GRANULE = 128
STEP = 100


beta_first = 0.9
beta_second = 0.95
epsilon = 1e-08
decay_rate = 0.1
learn_rate = 0.001


def shortened(shard):

    def short(part):
        return part.astype(jnp.bfloat16) if part.dtype == jnp.float32 else part

    return jax.tree.map(short, shard)


def build_window(pieces, flat_offsets, source, window_rows, full_width, n_fsdp):
    piece_count, granules, grain = pieces.shape
    row_granules = full_width // grain
    block_granules = row_granules // n_fsdp
    first_granule = flat_offsets[source * piece_count]
    last_granule = flat_offsets[source * piece_count + piece_count]
    row_first = first_granule * grain // full_width
    block_ids = jnp.arange(n_fsdp)[:, None, None]
    row_ids = jnp.arange(window_rows)[None, :, None]
    inner_ids = jnp.arange(block_granules)[None, None, :]
    granule_at = (
        row_first * row_granules + row_ids * row_granules + block_ids * block_granules + inner_ids
    )
    granule_at = granule_at.reshape(-1)
    which_piece = (granule_at >= flat_offsets[source * piece_count + 1]).astype(jnp.int32)
    piece_start = flat_offsets[source * piece_count + which_piece]
    inside = jnp.clip(granule_at - piece_start, 0, granules - 1)
    usable = (granule_at >= first_granule) & (granule_at < last_granule)
    table = pieces.reshape(piece_count * granules, grain)
    picked = jnp.take(table, which_piece * granules + inside, axis=0)
    return jnp.where(usable[:, None], picked, 0.0)


def as_columns(arrived, columns):
    return arrived.reshape(-1, columns)


def slot_fsdp(per_block, target_idx, sender_idx, slot_count):
    slot_ids = jnp.arange(slot_count)[None, :]
    return per_block * target_idx - 1 + slot_ids + (sender_idx == 0).astype(jnp.int32)


def spread_slots(arrived, n_fsdp, n_tp, tp_idx, window_rows):
    columns = arrived.shape[1]
    blocks = arrived.reshape(n_fsdp, window_rows, columns)
    per_block = n_fsdp // n_tp
    slot_count = per_block + 1
    targets = jnp.arange(n_tp)[:, None]
    src_fsdp = slot_fsdp(per_block, targets, tp_idx, slot_count)
    valid = (src_fsdp >= 0) & (src_fsdp < n_fsdp)
    picked = jnp.take(blocks, jnp.clip(src_fsdp, 0, n_fsdp - 1).reshape(-1), axis=0)
    picked = picked.reshape(n_tp, slot_count, window_rows, columns)
    return jnp.where(valid[:, :, None, None], picked, 0.0)


def place_rows(arrived, flat_offsets, n_fsdp, n_tp, tp_idx, rows_ff, piece_count, full_width):
    slot_count = arrived.shape[1]
    window_rows = arrived.shape[2]
    columns = arrived.shape[3]
    per_block = n_fsdp // n_tp
    senders = jnp.arange(n_tp)[:, None]
    src_fsdp = slot_fsdp(per_block, tp_idx, senders, slot_count)
    valid = (src_fsdp >= 0) & (src_fsdp < n_fsdp)
    src_device = jnp.clip(src_fsdp, 0, n_fsdp - 1) * n_tp + senders
    row_first = flat_offsets[src_device * piece_count] * GRANULE // full_width
    row_local = row_first[:, :, None] + jnp.arange(window_rows)[None, None, :] - tp_idx * rows_ff
    usable = valid[:, :, None] & (row_local >= 0) & (row_local < rows_ff)
    target_rows = jnp.where(usable, row_local, rows_ff).reshape(-1)
    placed = jnp.zeros((rows_ff, columns), jnp.float32)
    return placed.at[target_rows].add(arrived.reshape(-1, columns), mode="drop")


def train_step(master, hidden_acts, out_grad):
    weight = master.astype(jnp.bfloat16)
    grad_all = lax.all_gather(out_grad, "tp", axis=0, tiled=True)
    piece = lax.all_gather(hidden_acts, "fsdp", axis=0, tiled=True)
    grad_sum = lax.dot_general(
        piece, grad_all, (((0,), (0,)), ((), ())), preferred_element_type=jnp.float32
    )
    product = jnp.dot(piece, weight, preferred_element_type=jnp.float32)
    output = lax.psum_scatter(product.astype(jnp.bfloat16), "tp", scatter_dimension=0, tiled=True)
    return (output, grad_sum)


def adamw_update(master, momentum, variance, weight_grad):
    new_momentum = beta_first * momentum + (1.0 - beta_first) * weight_grad
    new_variance = beta_second * variance + (1.0 - beta_second) * weight_grad * weight_grad
    fix_first = 1.0 - beta_first**STEP
    fix_second = 1.0 - beta_second**STEP
    update = (
        new_momentum / fix_first / (jnp.sqrt(new_variance / fix_second) + epsilon)
        + decay_rate * master
    )
    return (master - learn_rate * update, new_momentum, new_variance)


def on_device(old_master, old_momentum, old_variance, flat_offsets, hidden_acts, out_grad):
    n_fsdp = lax.axis_size("fsdp")
    n_tp = lax.axis_size("tp")
    tp_idx = lax.axis_index("tp")
    fsdp_idx = lax.axis_index("fsdp")
    source = fsdp_idx * n_tp + tp_idx
    piece_count = old_master.shape[0]
    rows_ff = hidden_acts.shape[1]
    columns = out_grad.shape[1]
    full_width = columns * n_fsdp
    mean_piece = rows_ff * n_tp * full_width // (GRANULE * piece_count * n_fsdp * n_tp)
    jitter_most = mean_piece // 10
    window_rows = (piece_count * mean_piece + 2 * jitter_most) * GRANULE // full_width + 2

    def window_of(pieces):
        return build_window(pieces, flat_offsets, source, window_rows, full_width, n_fsdp)

    windows = (window_of(old_master), window_of(old_momentum), window_of(old_variance))
    master_cols, moment_cols, variance_cols = (
        lax.all_to_all(
            windows[0].astype(jnp.bfloat16), "fsdp", split_axis=0, concat_axis=0, tiled=True
        ).astype(jnp.float32),
        lax.all_to_all(
            windows[1].astype(jnp.bfloat16), "fsdp", split_axis=0, concat_axis=0, tiled=True
        ).astype(jnp.float32),
        lax.all_to_all(
            windows[2].astype(jnp.bfloat16), "fsdp", split_axis=0, concat_axis=0, tiled=True
        ).astype(jnp.float32),
    )
    master_cols = as_columns(master_cols, columns)
    moment_cols = as_columns(moment_cols, columns)
    variance_cols = as_columns(variance_cols, columns)
    master_arr, moment_arr, variance_arr = (
        lax.all_to_all(
            shortened(spread_slots(master_cols, n_fsdp, n_tp, tp_idx, window_rows)),
            "tp",
            split_axis=0,
            concat_axis=0,
            tiled=True,
        ),
        lax.all_to_all(
            shortened(spread_slots(moment_cols, n_fsdp, n_tp, tp_idx, window_rows)),
            "tp",
            split_axis=0,
            concat_axis=0,
            tiled=True,
        ),
        lax.all_to_all(
            shortened(spread_slots(variance_cols, n_fsdp, n_tp, tp_idx, window_rows)),
            "tp",
            split_axis=0,
            concat_axis=0,
            tiled=True,
        ),
    )
    master = place_rows(
        master_arr, flat_offsets, n_fsdp, n_tp, tp_idx, rows_ff, piece_count, full_width
    )
    momentum = place_rows(
        moment_arr, flat_offsets, n_fsdp, n_tp, tp_idx, rows_ff, piece_count, full_width
    )
    variance = place_rows(
        variance_arr, flat_offsets, n_fsdp, n_tp, tp_idx, rows_ff, piece_count, full_width
    )
    output, weight_grad = train_step(master, hidden_acts, out_grad)
    new_master, new_momentum, new_variance = adamw_update(master, momentum, variance, weight_grad)
    return (output, new_master, new_momentum, new_variance)


def solution(mesh):
    return jax.shard_map(
        on_device,
        mesh=mesh,
        in_specs=(
            P(("fsdp", "tp"), None, None),
            P(("fsdp", "tp"), None, None),
            P(("fsdp", "tp"), None, None),
            P(),
            P("fsdp", "tp"),
            P("tp", "fsdp"),
        ),
        out_specs=(P("tp", "fsdp"), P("tp", "fsdp"), P("tp", "fsdp"), P("tp", "fsdp")),
        check_vma=False,
    )
```

profile of v0, /device:TPU:1, one launch (start us, length us, event | category | flops | bytes accessed | tf_op | source)
XLA Modules:
  0.0 460.1 jit_solution(2375253247106061492)
XLA Ops:
  11.9 47.2 %gather_fusion.1 = s32[8000]{0:T(1024)S(1)} fusion(s32[257]{0:T(512)S(1)} %copy-done, s32[8192]{0:T(1024)S(1)} %pad_clamp_fusion.1), kind=kCustom, calls=%fused_computation.7 | custom fusion | bytes 96000 | tf_op jit(solution)/shard_map/gather | solution.py:40
  75.2 17.3 %gather_fusion.4 = bf16[8000,128]{1,0:T(8,128)(2,1)} fusion(bf16[8600,128]{1,0:T(8,128)(2,1)S(1)} %reshape.394, s32[8192]{0:T(1024)S(1)} %pad_clamp_fusion), kind=kCustom, calls=%fused_computation.2.clone | custom fusion | bytes 4128000 | tf_op jit(solution)/shard_map/jit(_take)/gather | solution.py:44
  92.5 17.6 %gather_fusion.2 = bf16[8000,128]{1,0:T(8,128)(2,1)} fusion(bf16[8600,128]{1,0:T(8,128)(2,1)} %reshape.392, s32[8192]{0:T(1024)S(1)} %pad_clamp_fusion), kind=kCustom, calls=%fused_computation.clone | custom fusion | bytes 4128000 | tf_op jit(solution)/shard_map/jit(_take)/gather | solution.py:44
  116.2 17.3 %gather_fusion.6 = bf16[8000,128]{1,0:T(8,128)(2,1)} fusion(bf16[8600,128]{1,0:T(8,128)(2,1)S(1)} %reshape.396, s32[8192]{0:T(1024)S(1)} %pad_clamp_fusion), kind=kCustom, calls=%fused_computation.3.clone | custom fusion | bytes 4128000 | tf_op jit(solution)/shard_map/jit(_take)/gather | solution.py:44
  133.5 11.3 %fusion = (bf16[8000,128]{1,0:T(8,128)(2,1)}, bf16[8000,128]{1,0:T(8,128)(2,1)S(1)}, bf16[8000,128]{1,0:T(8,128)(2,1)}) fusion(bf16[8000,128]{1,0:T(8,128)(2,1)} %gather_fusion.6, pred[8000]{0:T(1024)(128)(4,1)S(1)} %get-tuple-element.17, pred[8000]{0:T(1024)(128)(4,1)S(1)} %get-tuple-element.19, bf16[8000,128]{1,0:T(8,128)(2,1)} %gather_fusion.4, ...), kind=kLoop, calls=%fused_computation.16 | loop fusion | flops 6144000 | bytes 12304000 | tf_op jit(solution)/shard_map/convert_element_type | solution.py:137
  146.2 8.4 %all-to-all-start.2 = ((bf16[16,500,128]{2,1,0:T(8,128)(2,1)}), bf16[16,500,128]{2,1,0:T(8,128)(2,1)S(1)}, u32[]{:S(2)}, u32[]{:S(2)}) async-start(bf16[16,500,128]{2,1,0:T(8,128)(2,1)} %all_to_all.30), calls=%async_computation.3 | async-start | bytes 4128768 | tf_op jit(solution)/shard_map/all_to_all | solution.py:133
  158.3 23.7 %all-to-all-done.2 = bf16[16,500,128]{2,1,0:T(8,128)(2,1)S(1)} async-done(((bf16[16,500,128]{2,1,0:T(8,128)(2,1)}), bf16[16,500,128]{2,1,0:T(8,128)(2,1)S(1)}, u32[]{:S(2)}, u32[]{:S(2)}) %all-to-all-start.2) | async-done | bytes 2048032 | tf_op jit(solution)/shard_map/all_to_all | solution.py:133
  190.0 21.1 %all-to-all-done = bf16[16,500,128]{2,1,0:T(8,128)(2,1)} async-done(((bf16[16,500,128]{2,1,0:T(8,128)(2,1)}), bf16[16,500,128]{2,1,0:T(8,128)(2,1)}, u32[]{:S(2)}, u32[]{:S(2)}) %all-to-all-start) | async-done | bytes 2048032 | tf_op jit(solution)/shard_map/all_to_all | solution.py:130
  211.1 6.3 %all-to-all-start.4 = ((bf16[16,500,128]{2,1,0:T(8,128)(2,1)}), bf16[16,500,128]{2,1,0:T(8,128)(2,1)}, u32[]{:S(2)}, u32[]{:S(2)}) async-start(bf16[16,500,128]{2,1,0:T(8,128)(2,1)} %all_to_all.33), calls=%async_computation.5 | async-start | bytes 4128768 | tf_op jit(solution)/shard_map/all_to_all | solution.py:136
  229.0 11.7 %all-to-all-done.4 = bf16[16,500,128]{2,1,0:T(8,128)(2,1)} async-done(((bf16[16,500,128]{2,1,0:T(8,128)(2,1)}), bf16[16,500,128]{2,1,0:T(8,128)(2,1)}, u32[]{:S(2)}, u32[]{:S(2)}) %all-to-all-start.4) | async-done | bytes 2048032 | tf_op jit(solution)/shard_map/all_to_all | solution.py:136
  246.3 5.0 %broadcast_select_fusion = (bf16[24,125,512]{2,1,0:T(8,128)(2,1)S(1)}, bf16[24,125,512]{2,1,0:T(8,128)(2,1)S(1)}, bf16[24,125,512]{2,1,0:T(8,128)(2,1)S(1)}) fusion(bf16[24,125,512]{2,1,0:T(8,128)(2,1)} %gather_fusion.7, pred[24]{0:T(512)(128)(4,1)S(1)} %compare_and_fusion.2, bf16[24,125,512]{2,1,0:T(8,128)(2,1)} %gather_fusion.5, ...), kind=kLoop, calls=%fused_computation.24 | loop fusion | flops 4608000 | bytes 18432024 | tf_op jit(solution)/shard_map/jit(_take)/select_n | solution.py:65
  251.2 4.6 %select_convert_fusion = (bf16[8,3,125,512]{3,2,1,0:T(8,128)(2,1)}, bf16[8,3,125,512]{3,2,1,0:T(8,128)(2,1)}, bf16[8,3,125,512]{3,2,1,0:T(8,128)(2,1)S(1)}) fusion(bf16[8,3,125,512]{3,2,1,0:T(8,128)(2,1)S(1)} %bitcast.14, pred[8,3]{1,0:T(8,128)(4,1)S(1)} %fusion.17, bf16[8,3,125,512]{3,2,1,0:T(8,128)(2,1)S(1)} %bitcast.15, ...), kind=kLoop, calls=%fused_computation.11 | loop fusion | flops 4608000 | bytes 18432024 | tf_op jit(solution)/shard_map/convert_element_type | solution.py:20
  255.9 49.3 %all_to_all.42 = bf16[8,3,125,512]{3,2,1,0:T(8,128)(2,1)} all-to-all(bf16[8,3,125,512]{3,2,1,0:T(8,128)(2,1)S(1)} %get-tuple-element.30), channel_id=1, replica_groups=mesh['fsdp'=16,'tp'=8] {'tp'}, dimensions={0} | all-to-all | bytes 6144000 | tf_op jit(solution)/shard_map/all_to_all | solution.py:144
  305.2 4.6 all-to-all-start.3
  312.1 5.1 %reshape.472 = f32[3000,512]{1,0:T(8,128)} reshape(bf16[8,3,125,512]{3,2,1,0:T(8,128)(2,1)} %all_to_all.42) | data formatting | bytes 9216000 | tf_op jit(solution)/shard_map/convert_element_type | solution.py:84
  317.2 21.2 %scatter_custom_fusion = f32[1792,512]{1,0:T(8,128)} fusion(s32[3000]{0:T(1024)S(1)} %bitcast.17, f32[3000,512]{1,0:T(8,128)} %reshape.472, f32[]{:T(128)} %constant.46.clone.1), kind=kCustom, calls=%fused_computation.34 | custom fusion | flops 1536000 | bytes 3670528 | tf_op jit(solution)/shard_map/scatter-add | solution.py:84
  338.4 17.4 %all-to-all-done.3 = bf16[8,3,125,512]{3,2,1,0:T(8,128)(2,1)S(1)} async-done(((bf16[8,3,125,512]{3,2,1,0:T(8,128)(2,1)}), bf16[8,3,125,512]{3,2,1,0:T(8,128)(2,1)S(1)}, u32[]{:S(2)}, u32[]{:S(2)}) %all-to-all-start.3) | async-done | bytes 3072032 | tf_op jit(solution)/shard_map/all_to_all | solution.py:151
  355.8 5.2 %all-to-all-start.5 = ((bf16[8,3,125,512]{3,2,1,0:T(8,128)(2,1)}), bf16[8,3,125,512]{3,2,1,0:T(8,128)(2,1)}, u32[]{:S(2)}, u32[]{:S(2)}) async-start(bf16[8,3,125,512]{3,2,1,0:T(8,128)(2,1)} %get-tuple-element.28), calls=%async_computation.6 | async-start | bytes 6291456 | tf_op jit(solution)/shard_map/all_to_all | solution.py:158
  361.2 9.5 %fusion.4 = bf16[2048,512]{0,1:T(8,128)(2,1)} fusion(bf16[2048,1792]{1,0:T(8,128)(2,1)} %all-gather.3.cloned.1.call-done, f32[1792,512]{1,0:T(8,128)} %scatter_custom_fusion), kind=kOutput, calls=%fused_computation.28 | convolution fusion | flops 3760062464 | bytes 13107200 | tf_op jit(solution)/shard_map/dot_general | solution.py:94
  374.1 21.2 %scatter_custom_fusion.1 = f32[1792,512]{1,0:T(8,128)} fusion(s32[3000]{0:T(1024)S(1)} %bitcast.18, f32[3000,512]{1,0:T(8,128)} %reshape.480, f32[]{:T(128)} %constant.46.clone.1), kind=kCustom, calls=%fused_computation.32 | custom fusion | flops 1536000 | bytes 3670528 | tf_op jit(solution)/shard_map/scatter-add | solution.py:84
  395.3 12.0 %all-to-all-done.5 = bf16[8,3,125,512]{3,2,1,0:T(8,128)(2,1)} async-done(((bf16[8,3,125,512]{3,2,1,0:T(8,128)(2,1)}), bf16[8,3,125,512]{3,2,1,0:T(8,128)(2,1)}, u32[]{:S(2)}, u32[]{:S(2)}) %all-to-all-start.5) | async-done | bytes 3072032 | tf_op jit(solution)/shard_map/all_to_all | solution.py:158
  407.3 5.2 %reshape.488 = f32[3000,512]{1,0:T(8,128)} reshape(bf16[8,3,125,512]{3,2,1,0:T(8,128)(2,1)} %all-to-all-done.5) | data formatting | bytes 9216000 | tf_op jit(solution)/shard_map/convert_element_type | solution.py:84
  412.5 21.4 %scatter_custom_fusion.2 = f32[1792,512]{1,0:T(8,128)} fusion(s32[3000]{0:T(1024)S(1)} %bitcast.19, f32[3000,512]{1,0:T(8,128)} %reshape.488, f32[]{:T(128)} %constant.46.clone.1), kind=kCustom, calls=%fused_computation.30 | custom fusion | flops 1536000 | bytes 3670528 | tf_op jit(solution)/shard_map/scatter-add | solution.py:84
  433.9 17.6 %multiply_subtract_fusion = (f32[1792,512]{1,0:T(8,128)}, f32[1792,512]{1,0:T(8,128)}, f32[1792,512]{1,0:T(8,128)}) fusion(f32[1792,512]{1,0:T(8,128)} %scatter_custom_fusion, f32[1792,512]{1,0:T(8,128)} %scatter_custom_fusion.1, f32[1792,512]{1,0:T(8,128)} %scatter_custom_fusion.2, bf16[2048,1792]{1,0:T(8,128)(2,1)} %all-gather.3.cloned.1.call-done, ...), kind=kOutput, calls=%fused_computation.22 | convolution fusion | flops 3771858944 | bytes 31457280 | tf_op jit(solution)/shard_map/dot_general | solution.py:91
  (64 shorter events, 63.9 us)
Async XLA Ops:
  7.2 4.8 %copy-start = (s32[257]{0:T(512)S(1)}, s32[257]{0:T(512)}, u32[]{:S(2)}) copy-start(s32[257]{0:T(512)} %param.13) | copy-start | bytes 3088
  7.2 354.0 %all-gather.3.cloned.1.call-start = ((), (), s32[]{:S(2)}) async-start(), calls=%async_computation.7 | async-start | bytes 7798784 | tf_op jit(solution)/shard_map/all_gather | solution.py:90
  146.2 35.7 %all-to-all-start.2 = ((bf16[16,500,128]{2,1,0:T(8,128)(2,1)}), bf16[16,500,128]{2,1,0:T(8,128)(2,1)S(1)}, u32[]{:S(2)}, u32[]{:S(2)}) async-start(bf16[16,500,128]{2,1,0:T(8,128)(2,1)} %all_to_all.30), calls=%async_computation.3 | async-start | bytes 4128768 | tf_op jit(solution)/shard_map/all_to_all | solution.py:133
  182.0 8.1 %copy-start.1 = (bf16[16,500,128]{2,1,0:T(8,128)(2,1)}, bf16[16,500,128]{2,1,0:T(8,128)(2,1)S(1)}, u32[]{:S(2)}) copy-start(bf16[16,500,128]{2,1,0:T(8,128)(2,1)S(1)} %all-to-all-done.2) | copy-start | bytes 6144004
  182.0 29.2 %all-to-all-start = ((bf16[16,500,128]{2,1,0:T(8,128)(2,1)}), bf16[16,500,128]{2,1,0:T(8,128)(2,1)}, u32[]{:S(2)}, u32[]{:S(2)}) async-start(bf16[16,500,128]{2,1,0:T(8,128)(2,1)} %all_to_all.27), calls=%async_computation | async-start | bytes 4128768 | tf_op jit(solution)/shard_map/all_to_all | solution.py:130
  211.1 29.5 %all-to-all-start.4 = ((bf16[16,500,128]{2,1,0:T(8,128)(2,1)}), bf16[16,500,128]{2,1,0:T(8,128)(2,1)}, u32[]{:S(2)}, u32[]{:S(2)}) async-start(bf16[16,500,128]{2,1,0:T(8,128)(2,1)} %all_to_all.33), calls=%async_computation.5 | async-start | bytes 4128768 | tf_op jit(solution)/shard_map/all_to_all | solution.py:136
  305.2 50.6 %all-to-all-start.3 = ((bf16[8,3,125,512]{3,2,1,0:T(8,128)(2,1)}), bf16[8,3,125,512]{3,2,1,0:T(8,128)(2,1)S(1)}, u32[]{:S(2)}, u32[]{:S(2)}) async-start(bf16[8,3,125,512]{3,2,1,0:T(8,128)(2,1)} %get-tuple-element.29), calls=%async_computation.4 | async-start | bytes 6291456 | tf_op jit(solution)/shard_map/all_to_all | solution.py:151
  309.8 124.1 %all-gather.5.cloned.1.call-start = ((), (), s32[]{:S(2)}) async-start(), calls=%async_computation.9 | async-start | bytes 2359296 | tf_op jit(solution)/shard_map/all_gather | solution.py:89
  355.8 51.5 %all-to-all-start.5 = ((bf16[8,3,125,512]{3,2,1,0:T(8,128)(2,1)}), bf16[8,3,125,512]{3,2,1,0:T(8,128)(2,1)}, u32[]{:S(2)}, u32[]{:S(2)}) async-start(bf16[8,3,125,512]{3,2,1,0:T(8,128)(2,1)} %get-tuple-element.28), calls=%async_computation.6 | async-start | bytes 6291456 | tf_op jit(solution)/shard_map/all_to_all | solution.py:158
  361.0 90.6 %reduce-scatter.2.cloned.1.call-start = ((), (), s32[]{:S(2)}) async-start(), calls=%async_computation.8 | async-start | bytes 2359296 | tf_op jit(solution)/shard_map/reduce_scatter | solution.py:95
Sparse Core Ops, SparseCore 0:
  10.2 69.4 all-gather.2
  312.3 31.5 all-gather.4
  370.9 39.4 reduce-scatter.1
where the time goes:
time: 468 us; the launch traced here: 460 us
  local copies, waits for them, and re-layouts  164 us (35%)
  other arithmetic  88.5 us (19%)
  waiting for transfers between devices  87.3 us (19%)
  blocking collectives  49.3 us (11%)
  starting transfers between devices  29.2 us (6%)
  matrix products  27.2 us (6%)
  between operations  14.9 us (3%)
    scatter-add x3, other arithmetic, place_rows(): return placed.at[target_rows].add(arrived.reshape(-1, columns), mode='drop')  63.9 us
    gather x3, local copies, waits for them, and re-layouts, build_window(): picked = jnp.take(table, which_piece * granules + inside, axis=0)  52.2 us
    all_to_all x1, blocking collectives, on_device(): lax.all_to_all(shortened(spread_slots(master_cols, n_fsdp, n_tp, tp_idx,...  49.3 us
    gather x1, local copies, waits for them, and re-layouts, build_window(): piece_start = flat_offsets[source * piece_count + which_piece]  47.2 us
    all_to_all x1, waiting for transfers between devices, on_device(): lax.all_to_all(windows[1].astype(jnp.bfloat16), 'fsdp', split_axis=0, con...  23.7 us
    all_to_all x1, waiting for transfers between devices, on_device(): lax.all_to_all(windows[0].astype(jnp.bfloat16), 'fsdp', split_axis=0, con...  21.1 us
    dot_general x1, matrix products, train_step(): lax.dot_general(piece, grad_all, (((0,), (0,)), ((), ())), preferred_elem...  17.6 us
    all_to_all x1, waiting for transfers between devices, on_device(): lax.all_to_all(shortened(spread_slots(moment_cols, n_fsdp, n_tp, tp_idx,...  17.4 us
  transfers between devices with their start and end apart: 8, of which 5 were waited for; matrix products, arithmetic and copies ran while one was open for 58% of the time, Pallas kernels for 0%

commit v1 on v0

v1 whole, which is shorter than its diff:
```python
import functools

import jax
import jax.numpy as jnp
from jax import lax
from jax.experimental import pallas as pl
from jax.experimental.pallas import tpu as pltpu
from jax.sharding import PartitionSpec as P

LANES = 128
STEP = 100
AXES = ("fsdp", "tp")
N_FSDP, N_TP = 16, 8
N_ALL = N_FSDP * N_TP
ROW_GRANULES = 64
ROWS = 112
OWN = ROWS * ROW_GRANULES
COLS = 512
ROUNDS = 16
EDGE = 384
GRAN = 4300
TABLE = 2 * GRAN
FRONT = 1792
BACK = 1080

beta_first = 0.9
beta_second = 0.95
epsilon = 1e-08
decay_rate = 0.1
learn_rate = 0.001

PHASES = ((0,), (1, 2))


def source_of(f, t):
    return f * N_TP + t


def target_column(round_id, f, t):
    rx, rz = divmod(round_id, 4)
    x, z, y, c = f // 4, f % 4, t // 2, t % 2
    return ((x + rx + 4 - y + 2 * c) % 4) * 4 + (z + 2 * c + rz) % 4


def sender_block(round_id, f, t):
    rx, rz = divmod(round_id, 4)
    xp, zp, yp, cp = f // 4, f % 4, t // 2, t % 2
    w = (zp + 8 - 2 * cp - rz) % 4
    b, c = w % 2, w // 2
    y = (yp + rx + 2 * c + 4 - xp) % 4
    return b * N_TP + y * 2 + c


def round_pairs(round_id):
    pairs = []
    for f in range(N_FSDP):
        for t in range(N_TP):
            pairs.append((source_of(f, t), source_of(target_column(round_id, f, t), f // 2)))
    return pairs


def edge_kernel(flat, *refs):
    tables, (to_left, to_right) = refs[:3], refs[3:5]
    heads, tails, sems = refs[5:]
    copies = []
    for k in range(3):
        head = pltpu.make_async_copy(
            tables[k].at[pl.ds(0, 768)], heads.at[k, pl.ds(1536, 768)], sems.at[k, 0]
        )
        tail = pltpu.make_async_copy(
            tables[k].at[pl.ds(6448, 2152)], tails.at[k, pl.ds(0, 2152)], sems.at[k, 1]
        )
        head.start()
        tail.start()
        copies.append((head, tail))
    s = source_of(lax.axis_index("fsdp"), lax.axis_index("tp"))
    nominal = s * OWN
    first, middle, last = flat[2 * s], flat[2 * s + 1], flat[2 * s + 2]
    ids = lax.broadcasted_iota(jnp.int32, (EDGE, LANES), 0)
    left_at = nominal - EDGE - first
    right_at = nominal + OWN - middle
    left_ok = ids + left_at >= 0
    right_ok = ids + right_at < last - middle
    for k in range(3):
        copies[k][0].wait()
        copies[k][1].wait()
        left = heads[k, pl.ds(1536 + 2 * left_at, EDGE, stride=2), :]
        right = tails[k, pl.ds(2 * right_at + 1 - 6448, EDGE, stride=2), :]
        to_left[k * EDGE : (k + 1) * EDGE, :] = jnp.where(left_ok, left, 0.0).astype(jnp.bfloat16)
        to_right[k * EDGE : (k + 1) * EDGE, :] = jnp.where(right_ok, right, 0.0).astype(
            jnp.bfloat16
        )


def pack_kernel(which, flat, *refs):
    count = len(which)
    tables = refs[:count]
    from_left, from_right = refs[count : count + 2]
    outs = refs[count + 2 : count + 2 + ROUNDS]
    held, left_edge, right_edge, sems = refs[count + 2 + ROUNDS :]
    copies = []
    for k in range(count):
        copy = pltpu.make_async_copy(
            tables[k], held.at[k, pl.ds(FRONT, TABLE)], sems.at[k]
        )
        copy.start()
        copies.append(copy)
    f, t = lax.axis_index("fsdp"), lax.axis_index("tp")
    s = source_of(f, t)
    nominal = s * OWN
    low = flat[2 * s] - nominal
    cut = flat[2 * s + 1] - nominal
    high = flat[2 * s + 2] - nominal
    for k in range(count):
        at = which[k] * EDGE
        left_edge[k, 0:EDGE, :] = from_left[at : at + EDGE, :].astype(jnp.float32)
        right_edge[k, 1024 - EDGE : 1024, :] = from_right[at : at + EDGE, :].astype(jnp.float32)
    ids = lax.broadcasted_iota(jnp.int32, (16, LANES), 0) * ROW_GRANULES
    stride = 2 * ROW_GRANULES
    for k in range(count):
        copies[k].wait()
        for r in range(ROUNDS):
            column = target_column(r, f, t) * 4
            for q in range(4):
                c = column + q
                at_a = FRONT + 2 * (c - low)
                at_b = FRONT + 2 * (c - cut) + 1

                def rows_of(at, row, n):
                    return held[k, pl.ds(at + row * stride, n, stride=stride), :]

                def put(row, n, value):
                    outs[r][k * ROWS + row : k * ROWS + row + n, q * LANES : (q + 1) * LANES] = (
                        value.astype(jnp.bfloat16)
                    )

                edge = left_edge[k, pl.ds(c, 16, stride=ROW_GRANULES), :]
                put(0, 16, jnp.where(ids + c < low, edge, rows_of(at_a, 0, 16)))
                put(16, 32, rows_of(at_a, 16, 32))
                put(
                    48,
                    16,
                    jnp.where(
                        ids + c + 48 * ROW_GRANULES < cut,
                        rows_of(at_a, 48, 16),
                        rows_of(at_b, 48, 16),
                    ),
                )
                put(64, 32, rows_of(at_b, 64, 32))
                edge = right_edge[k, pl.ds(c, 16, stride=ROW_GRANULES), :]
                put(
                    96,
                    16,
                    jnp.where(ids + c + 96 * ROW_GRANULES >= high, edge, rows_of(at_b, 96, 16)),
                )


def product_kernel(acts, *refs):
    parts, out, weight = refs[:ROUNDS], refs[ROUNDS], refs[ROUNDS + 1]

    @pl.when(pl.program_id(0) == 0)
    def _():
        f, t = lax.axis_index("fsdp"), lax.axis_index("tp")
        for r in range(ROUNDS):
            at = pl.multiple_of(sender_block(r, f, t) * ROWS, 16)
            weight[pl.ds(at, ROWS), :] = parts[r][...]

    out[...] = jnp.dot(acts[...], weight[...], preferred_element_type=jnp.float32).astype(
        jnp.bfloat16
    )


def update_kernel(where, *refs):
    n_phase = 1 + max(phase for phase, _ in where)
    arrived = [refs[p * ROUNDS : (p + 1) * ROUNDS] for p in range(n_phase)]
    at = n_phase * ROUNDS
    grad = refs[at]
    new_master, new_momentum, new_variance = refs[at + 1 : at + 4]
    held, grads, results, in_sems, out_sems = refs[at + 4 :]
    f, t = lax.axis_index("fsdp"), lax.axis_index("tp")
    rows = [pl.multiple_of(sender_block(r, f, t) * ROWS, 16) for r in range(ROUNDS)]
    copies = []
    for r in range(ROUNDS):
        mine = []
        for k in range(3):
            phase, row = where[k]
            mine.append(
                pltpu.make_async_copy(
                    arrived[phase][r].at[pl.ds(row, ROWS)], held.at[r, k], in_sems.at[r, k]
                )
            )
        mine.append(
            pltpu.make_async_copy(grad.at[pl.ds(rows[r], ROWS)], grads.at[r], in_sems.at[r, 3])
        )
        for copy in mine:
            copy.start()
        copies.append(mine)
    fix_first = 1.0 - beta_first**STEP
    fix_second = 1.0 - beta_second**STEP
    leaving = []
    for r in range(ROUNDS):
        for copy in copies[r]:
            copy.wait()
        master = held[r, 0].astype(jnp.float32)
        momentum = held[r, 1].astype(jnp.float32)
        variance = held[r, 2].astype(jnp.float32)
        g = grads[r]
        m = beta_first * momentum + (1.0 - beta_first) * g
        v = beta_second * variance + (1.0 - beta_second) * g * g
        update = m / fix_first / (jnp.sqrt(v / fix_second) + epsilon) + decay_rate * master
        results[r, 0] = master - learn_rate * update
        results[r, 1] = m
        results[r, 2] = v
        for k, out in enumerate((new_master, new_momentum, new_variance)):
            copy = pltpu.make_async_copy(
                results.at[r, k], out.at[pl.ds(rows[r], ROWS)], out_sems.at[r, k]
            )
            copy.start()
            leaving.append(copy)
    for copy in leaving:
        copy.wait()


def any_spec():
    return pl.BlockSpec(memory_space=pl.ANY)


def smem_spec():
    return pl.BlockSpec(memory_space=pltpu.SMEM)


def vmem_spec():
    return pl.BlockSpec(memory_space=pltpu.VMEM)


def make_edges(flat, tables):
    shape = jax.ShapeDtypeStruct((3 * EDGE, LANES), jnp.bfloat16)
    return pl.pallas_call(
        edge_kernel,
        out_shape=(shape, shape),
        in_specs=[smem_spec()] + [any_spec()] * 3,
        out_specs=(vmem_spec(), vmem_spec()),
        scratch_shapes=[
            pltpu.VMEM((3, 2304, LANES), jnp.float32),
            pltpu.VMEM((3, 2240, LANES), jnp.float32),
            pltpu.SemaphoreType.DMA((3, 2)),
        ],
        compiler_params=pltpu.CompilerParams(vmem_limit_bytes=24 * 2**20),
        cost_estimate=pl.CostEstimate(flops=0, bytes_accessed=6 * 2**20, transcendentals=0),
        name="edges",
    )(flat, *tables)


def make_messages(which, flat, tables, from_left, from_right):
    count = len(which)
    shape = jax.ShapeDtypeStruct((count * ROWS, COLS), jnp.bfloat16)
    return pl.pallas_call(
        functools.partial(pack_kernel, which),
        out_shape=(shape,) * ROUNDS,
        in_specs=[smem_spec()] + [any_spec()] * count + [vmem_spec()] * 2,
        out_specs=(vmem_spec(),) * ROUNDS,
        scratch_shapes=[
            pltpu.VMEM((count, FRONT + TABLE + BACK, LANES), jnp.float32),
            pltpu.VMEM((count, 1024, LANES), jnp.float32),
            pltpu.VMEM((count, 1024, LANES), jnp.float32),
            pltpu.SemaphoreType.DMA((count,)),
        ],
        compiler_params=pltpu.CompilerParams(vmem_limit_bytes=40 * 2**20),
        cost_estimate=pl.CostEstimate(
            flops=0, bytes_accessed=count * 7 * 2**20, transcendentals=0
        ),
        name="pack",
    )(flat, *[tables[k] for k in which], from_left, from_right)


def make_product(acts, parts):
    tokens, depth = acts.shape
    tile = 256
    return pl.pallas_call(
        product_kernel,
        out_shape=jax.ShapeDtypeStruct((tokens, COLS), jnp.bfloat16),
        grid=(tokens // tile,),
        in_specs=[pl.BlockSpec((tile, depth), lambda i: (i, 0))]
        + [pl.BlockSpec((ROWS, COLS), lambda i: (0, 0))] * ROUNDS,
        out_specs=pl.BlockSpec((tile, COLS), lambda i: (i, 0)),
        scratch_shapes=[pltpu.VMEM((depth, COLS), jnp.bfloat16)],
        compiler_params=pltpu.CompilerParams(vmem_limit_bytes=24 * 2**20),
        cost_estimate=pl.CostEstimate(
            flops=2 * tokens * depth * COLS, bytes_accessed=12 * 2**20, transcendentals=0
        ),
        name="product",
    )(acts, *parts)


def make_update(arrived, where, grad):
    shape = jax.ShapeDtypeStruct(grad.shape, jnp.float32)
    return pl.pallas_call(
        functools.partial(update_kernel, where),
        out_shape=(shape,) * 3,
        in_specs=[any_spec()] * (len(arrived) * ROUNDS + 1),
        out_specs=(any_spec(),) * 3,
        scratch_shapes=[
            pltpu.VMEM((ROUNDS, 3, ROWS, COLS), jnp.bfloat16),
            pltpu.VMEM((ROUNDS, ROWS, COLS), jnp.float32),
            pltpu.VMEM((ROUNDS, 3, ROWS, COLS), jnp.float32),
            pltpu.SemaphoreType.DMA((ROUNDS, 4)),
            pltpu.SemaphoreType.DMA((ROUNDS, 3)),
        ],
        compiler_params=pltpu.CompilerParams(vmem_limit_bytes=32 * 2**20),
        cost_estimate=pl.CostEstimate(
            flops=30 * grad.size, bytes_accessed=20 * 2**20, transcendentals=0
        ),
        name="update",
    )(*[a for phase in arrived for a in phase], grad)


def on_device(old_master, old_momentum, old_variance, flat_offsets, hidden_acts, out_grad):
    acts = lax.all_gather(hidden_acts, "fsdp", axis=0, tiled=True)
    tables = [
        jnp.transpose(old, (1, 0, 2)).reshape(TABLE, LANES)
        for old in (old_master, old_momentum, old_variance)
    ]
    to_left, to_right = make_edges(flat_offsets, tables)
    from_left = lax.ppermute(to_right, AXES, [(s, (s + 1) % N_ALL) for s in range(N_ALL)])
    from_right = lax.ppermute(to_left, AXES, [(s, (s - 1) % N_ALL) for s in range(N_ALL)])
    arrived = []
    where = [None] * 3
    for number, which in enumerate(PHASES):
        messages = make_messages(which, flat_offsets, tables, from_left, from_right)
        arrived.append(
            [lax.ppermute(messages[r], AXES, round_pairs(r)) for r in range(ROUNDS)]
        )
        for k, tensor in enumerate(which):
            where[tensor] = (number, k * ROWS)
    grads_out = lax.all_gather(out_grad, "tp", axis=0, tiled=True)
    product = make_product(acts, arrived[0])
    output = lax.psum_scatter(product, "tp", scatter_dimension=0, tiled=True)
    weight_grad = lax.dot_general(
        acts, grads_out, (((0,), (0,)), ((), ())), preferred_element_type=jnp.float32
    )
    new_master, new_momentum, new_variance = make_update(arrived, where, weight_grad)
    return (output, new_master, new_momentum, new_variance)


def solution(mesh):
    return jax.shard_map(
        on_device,
        mesh=mesh,
        in_specs=(
            P(("fsdp", "tp"), None, None),
            P(("fsdp", "tp"), None, None),
            P(("fsdp", "tp"), None, None),
            P(),
            P("fsdp", "tp"),
            P("tp", "fsdp"),
        ),
        out_specs=(P("tp", "fsdp"), P("tp", "fsdp"), P("tp", "fsdp"), P("tp", "fsdp")),
        check_vma=False,
    )
```

time: 468 us -> 218 us (0.47)
  local copies, waits for them, and re-layouts: 164 us -> 15.3 us
  starting transfers between devices: 29.2 us -> 121 us
  other arithmetic: 88.5 us -> 0.01 us
  waiting for transfers between devices: 87.3 us -> 15.3 us
  blocking collectives: 49.3 us -> 0 us
  Pallas kernels: 0 us -> 41 us
  matrix products: 27.2 us -> 7.07 us
    ppermute x0 -> x34, starting transfers between devices: none -> 121 us  [the longest x32 118 us: on_device(): lax.ppermute(messages[r], AXES, round_pairs(r))]
    gather x8 -> x0, local copies, waits for them, and re-layouts: 108 us -> none  [the longest x3 52.2 us: build_window(): picked = jnp.take(table, which_piece * granules + inside, axis=0)]
    all_to_all x5 -> x0, waiting for transfers between devices: 85.9 us -> none  [the longest x1 23.7 us: on_device(): lax.all_to_all(windows[1].astype(jnp.bfloat16), 'fsdp', split_axis=0, con...]
    scatter-add x3 -> x0, other arithmetic: 63.9 us -> none  [place_rows(): return placed.at[target_rows].add(arrived.reshape(-1, columns), mode='drop')]
    all_to_all x1 -> x0, blocking collectives: 49.3 us -> none  [on_device(): lax.all_to_all(shortened(spread_slots(master_cols, n_fsdp, n_tp, tp_idx,...]
    pallas_call x0 -> x5, Pallas kernels: none -> 41 us  [the longest x1 18.4 us: make_update(): pl.pallas_call(functools.partial(update_kernel, where), out_shape=(shape,...]
    all_to_all x5 -> x0, starting transfers between devices: 28.9 us -> none  [the longest x1 8.42 us: on_device(): lax.all_to_all(windows[1].astype(jnp.bfloat16), 'fsdp', split_axis=0, con...]
    convert_element_type x6 -> x0, local copies, waits for them, and re-layouts: 22.9 us -> none  [the longest x3 13.6 us: place_rows(): return placed.at[target_rows].add(arrived.reshape(-1, columns), mode='drop')]
  transfers between devices with their start and end apart: 8 -> 37, of which waited for: 5 -> 6; matrix products, arithmetic and copies ran while one was open for 58% -> 3% of each run, Pallas kernels for 0% -> 19%
where the time goes in v1:
time: 218 us; the launch traced here: 214 us
  starting transfers between devices  121 us (56%)
  Pallas kernels  41 us (19%)
  local copies, waits for them, and re-layouts  15.3 us (7%)
  waiting for transfers between devices  15.3 us (7%)
  between operations  14.5 us (7%)
  matrix products  7.07 us (3%)
    ppermute x32, starting transfers between devices, on_device(): lax.ppermute(messages[r], AXES, round_pairs(r))  118 us
    pallas_call x1, Pallas kernels, make_update(): pl.pallas_call(functools.partial(update_kernel, where), out_shape=(shape,...  18.4 us
    unnamed x80, local copies, waits for them, and re-layouts  15.3 us
    pallas_call x2, Pallas kernels, make_messages(): pl.pallas_call(functools.partial(pack_kernel, which), out_shape=(shape,)...  14.5 us
    dot_general x1, matrix products, on_device(): lax.dot_general(acts, grads_out, (((0,), (0,)), ((), ())), preferred_elem...  7.07 us
    pallas_call x1, Pallas kernels, make_product(): pl.pallas_call(product_kernel, out_shape=jax.ShapeDtypeStruct((tokens, CO...  6.32 us
  transfers between devices with their start and end apart: 37, of which 6 were waited for; matrix products, arithmetic and copies ran while one was open for 3% of the time, Pallas kernels for 19%

profile of v1, /device:TPU:1, one launch (start us, length us, event | category | flops | bytes accessed | tf_op | source)
XLA Modules:
  0.0 214.3 jit_solution(17857292487436861318)
XLA Ops:
  20.6 3.7 %collective-permute-done.refs_1_.refs_2_ = bf16[1152,128]{1,0:T(8,128)(2,1)S(1)} collective-permute-done((bf16[1152,128]{1,0:T(8,128)(2,1)S(1)}, bf16[1152,128]{1,0:T(8,128)(2,1)S(1)}, u32[]{:S(2)}, u32[]{:S(2)}) %collective-permute-start) | collective-permute-done | bytes 294944 | tf_op jit(solution)/shard_map/ppermute | solution.py:324
  27.2 4.6 %pack.2 = (bf16[112,512]{1,0:T(8,128)(2,1)S(1)}, bf16[112,512]{1,0:T(8,128)(2,1)S(1)}, bf16[112,512]{1,0:T(8,128)(2,1)S(1)}, bf16[112,512]{1,0:T(8,128)(2,1)S(1)...) custom-call(s32[257]{0:T(512)S(1)} %copy-done.36, ...), custom_call_target="tpu_custom_call" | custom-call | bytes 7340032 | tf_op jit(solution)/shard_map/pack/pallas_call | solution.py:257
  31.8 8.5 %collective-permute-start.2 = (bf16[112,512]{1,0:T(8,128)(2,1)S(1)}, bf16[112,512]{1,0:T(8,128)(2,1)S(1)}, u32[]{:S(2)}, u32[]{:S(2)}) collective-permute-start(bf16[112,512]{1,0:T(8,128)(2,1)S(1)} %get-tuple-element.43), channel_id=1, source_target_pairs={{0,0},{1,80},{2,96},{3,48},{4,64},{5,16},{6,32},{7,112},{8,8},{9,8... | collective-permute-start | bytes 344072 | tf_op jit(solution)/shard_map/ppermute | solution.py:331
  44.8 3.7 %collective-permute-start.5 = (bf16[112,512]{1,0:T(8,128)(2,1)S(1)}, bf16[112,512]{1,0:T(8,128)(2,1)S(1)}, u32[]{:S(2)}, u32[]{:S(2)}) collective-permute-start(bf16[112,512]{1,0:T(8,128)(2,1)S(1)} %get-tuple-element.46), channel_id=1, source_target_pairs={{0,24},{1,72},{2,120},{3,40},{4,88},{5,8},{6,56},{7,104},{8,0},{9,... | collective-permute-start | bytes 344072 | tf_op jit(solution)/shard_map/ppermute | solution.py:331
  48.5 4.4 %collective-permute-start.6 = (bf16[112,512]{1,0:T(8,128)(2,1)S(1)}, bf16[112,512]{1,0:T(8,128)(2,1)S(1)}, u32[]{:S(2)}, u32[]{:S(2)}) collective-permute-start(bf16[112,512]{1,0:T(8,128)(2,1)S(1)} %get-tuple-element.47), channel_id=1, source_target_pairs={{0,32},{1,112},{2,0},{3,80},{4,96},{5,48},{6,64},{7,16},{8,40},{9,... | collective-permute-start | bytes 344072 | tf_op jit(solution)/shard_map/ppermute | solution.py:331
  53.0 3.7 %collective-permute-start.7 = (bf16[112,512]{1,0:T(8,128)(2,1)S(1)}, bf16[112,512]{1,0:T(8,128)(2,1)S(1)}, u32[]{:S(2)}, u32[]{:S(2)}) collective-permute-start(bf16[112,512]{1,0:T(8,128)(2,1)S(1)} %get-tuple-element.48), channel_id=1, source_target_pairs={{0,40},{1,120},{2,8},{3,88},{4,104},{5,56},{6,72},{7,24},{8,48},{9... | collective-permute-start | bytes 344072 | tf_op jit(solution)/shard_map/ppermute | solution.py:331
  56.6 5.4 %collective-permute-start.8 = (bf16[112,512]{1,0:T(8,128)(2,1)S(1)}, bf16[112,512]{1,0:T(8,128)(2,1)S(1)}, u32[]{:S(2)}, u32[]{:S(2)}) collective-permute-start(bf16[112,512]{1,0:T(8,128)(2,1)S(1)} %get-tuple-element.49), channel_id=1, source_target_pairs={{0,48},{1,96},{2,16},{3,64},{4,112},{5,32},{6,80},{7,0},{8,56},{9,... | collective-permute-start | bytes 344072 | tf_op jit(solution)/shard_map/ppermute | solution.py:331
  68.6 5.0 %collective-permute-start.12 = (bf16[112,512]{1,0:T(8,128)(2,1)S(1)}, bf16[112,512]{1,0:T(8,128)(2,1)S(1)}, u32[]{:S(2)}, u32[]{:S(2)}) collective-permute-start(bf16[112,512]{1,0:T(8,128)(2,1)S(1)} %get-tuple-element.53), channel_id=1, source_target_pairs={{0,80},{1,0},{2,48},{3,96},{4,16},{5,64},{6,112},{7,32},{8,88},{9,... | collective-permute-start | bytes 344072 | tf_op jit(solution)/shard_map/ppermute | solution.py:331
  73.6 4.9 %collective-permute-start.13 = (bf16[112,512]{1,0:T(8,128)(2,1)S(1)}, bf16[112,512]{1,0:T(8,128)(2,1)S(1)}, u32[]{:S(2)}, u32[]{:S(2)}) collective-permute-start(bf16[112,512]{1,0:T(8,128)(2,1)S(1)} %get-tuple-element.54), channel_id=1, source_target_pairs={{0,88},{1,8},{2,56},{3,104},{4,24},{5,72},{6,120},{7,40},{8,64},{9... | collective-permute-start | bytes 344072 | tf_op jit(solution)/shard_map/ppermute | solution.py:331
  82.4 4.8 %collective-permute-start.16 = (bf16[112,512]{1,0:T(8,128)(2,1)S(1)}, bf16[112,512]{1,0:T(8,128)(2,1)S(1)}, u32[]{:S(2)}, u32[]{:S(2)}) collective-permute-start(bf16[112,512]{1,0:T(8,128)(2,1)S(1)} %get-tuple-element.57), channel_id=1, source_target_pairs={{0,112},{1,32},{2,80},{3,0},{4,48},{5,96},{6,16},{7,64},{8,120},{9... | collective-permute-start | bytes 344072 | tf_op jit(solution)/shard_map/ppermute | solution.py:331
  87.3 5.3 %collective-permute-start.17 = (bf16[112,512]{1,0:T(8,128)(2,1)S(1)}, bf16[112,512]{1,0:T(8,128)(2,1)S(1)}, u32[]{:S(2)}, u32[]{:S(2)}) collective-permute-start(bf16[112,512]{1,0:T(8,128)(2,1)S(1)} %get-tuple-element.58), channel_id=1, source_target_pairs={{0,120},{1,40},{2,88},{3,8},{4,56},{5,104},{6,24},{7,72},{8,96},{9... | collective-permute-start | bytes 344072 | tf_op jit(solution)/shard_map/ppermute | solution.py:331
  100.6 6.3 %product.1 = bf16[2048,512]{1,0:T(8,128)(2,1)} custom-call(bf16[2048,1792]{1,0:T(8,128)(2,1)S(1)} %copy-done.37, bf16[112,512]{1,0:T(8,128)(2,1)S(1)} %collective-permute-done.2.refs_0_, bf16[112,512]{1,0:T(8,128)(2,1)S(1)} %collective-permute-done.3.refs_1_, bf16[112,512]{1,0:T(8,128)(2,1)S(1)} %collective-permute-done.4.refs_2_, ...), custom_call_target="tpu_custom_call" | custom-call | flops 3758096384 | bytes 12582912 | tf_op jit(solution)/shard_map/product/pallas_call | solution.py:279
  111.8 9.9 %pack.3 = (bf16[224,512]{1,0:T(8,128)(2,1)S(1)}, bf16[224,512]{1,0:T(8,128)(2,1)S(1)}, bf16[224,512]{1,0:T(8,128)(2,1)S(1)}, bf16[224,512]{1,0:T(8,128)(2,1)S(1)...) custom-call(s32[257]{0:T(512)S(1)} %copy-done.36, ...), custom_call_target="tpu_custom_call" | custom-call | bytes 14680064 | tf_op jit(solution)/shard_map/pack/pallas_call | solution.py:257
  121.7 7.1 %collective-permute-start.18 = (bf16[224,512]{1,0:T(8,128)(2,1)S(1)}, bf16[224,512]{1,0:T(8,128)(2,1)S(1)}, u32[]{:S(2)}, u32[]{:S(2)}) collective-permute-start(bf16[224,512]{1,0:T(8,128)(2,1)S(1)} %get-tuple-element.59), channel_id=1, source_target_pairs={{0,0},{1,80},{2,96},{3,48},{4,64},{5,16},{6,32},{7,112},{8,8},{9,8... | collective-permute-start | bytes 688136 | tf_op jit(solution)/shard_map/ppermute | solution.py:331
  130.7 3.9 %collective-permute-start.20 = (bf16[224,512]{1,0:T(8,128)(2,1)S(1)}, bf16[224,512]{1,0:T(8,128)(2,1)S(1)}, u32[]{:S(2)}, u32[]{:S(2)}) collective-permute-start(bf16[224,512]{1,0:T(8,128)(2,1)S(1)} %get-tuple-element.61), channel_id=1, source_target_pairs={{0,16},{1,64},{2,112},{3,32},{4,80},{5,0},{6,48},{7,96},{8,24},{9,... | collective-permute-start | bytes 688136 | tf_op jit(solution)/shard_map/ppermute | solution.py:331
  135.7 5.8 %collective-permute-start.22 = (bf16[224,512]{1,0:T(8,128)(2,1)S(1)}, bf16[224,512]{1,0:T(8,128)(2,1)S(1)}, u32[]{:S(2)}, u32[]{:S(2)}) collective-permute-start(bf16[224,512]{1,0:T(8,128)(2,1)S(1)} %get-tuple-element.63), channel_id=1, source_target_pairs={{0,32},{1,112},{2,0},{3,80},{4,96},{5,48},{6,64},{7,16},{8,40},{9,... | collective-permute-start | bytes 688136 | tf_op jit(solution)/shard_map/ppermute | solution.py:331
  141.5 3.6 %collective-permute-start.23 = (bf16[224,512]{1,0:T(8,128)(2,1)S(1)}, bf16[224,512]{1,0:T(8,128)(2,1)S(1)}, u32[]{:S(2)}, u32[]{:S(2)}) collective-permute-start(bf16[224,512]{1,0:T(8,128)(2,1)S(1)} %get-tuple-element.64), channel_id=1, source_target_pairs={{0,40},{1,120},{2,8},{3,88},{4,104},{5,56},{6,72},{7,24},{8,48},{9... | collective-permute-start | bytes 688136 | tf_op jit(solution)/shard_map/ppermute | solution.py:331
  145.2 7.1 %collective-permute-start.24 = (bf16[224,512]{1,0:T(8,128)(2,1)S(1)}, bf16[224,512]{1,0:T(8,128)(2,1)S(1)}, u32[]{:S(2)}, u32[]{:S(2)}) collective-permute-start(bf16[224,512]{1,0:T(8,128)(2,1)S(1)} %get-tuple-element.65), channel_id=1, source_target_pairs={{0,48},{1,96},{2,16},{3,64},{4,112},{5,32},{6,80},{7,0},{8,56},{9,... | collective-permute-start | bytes 688136 | tf_op jit(solution)/shard_map/ppermute | solution.py:331
  156.9 6.7 %collective-permute-start.28 = (bf16[224,512]{1,0:T(8,128)(2,1)S(1)}, bf16[224,512]{1,0:T(8,128)(2,1)S(1)}, u32[]{:S(2)}, u32[]{:S(2)}) collective-permute-start(bf16[224,512]{1,0:T(8,128)(2,1)S(1)} %get-tuple-element.69), channel_id=1, source_target_pairs={{0,80},{1,0},{2,48},{3,96},{4,16},{5,64},{6,112},{7,32},{8,88},{9,... | collective-permute-start | bytes 688136 | tf_op jit(solution)/shard_map/ppermute | solution.py:331
  163.5 5.1 %collective-permute-start.29 = (bf16[224,512]{1,0:T(8,128)(2,1)}, bf16[224,512]{1,0:T(8,128)(2,1)S(1)}, u32[]{:S(2)}, u32[]{:S(2)}) collective-permute-start(bf16[224,512]{1,0:T(8,128)(2,1)} %get-tuple-element.70), channel_id=1, source_target_pairs={{0,88},{1,8},{2,56},{3,104},{4,24},{5,72},{6,120},{7,40},{8,64},{9... | collective-permute-start | bytes 688136 | tf_op jit(solution)/shard_map/ppermute | solution.py:331
  173.2 4.0 %collective-permute-start.32 = (bf16[224,512]{1,0:T(8,128)(2,1)}, bf16[224,512]{1,0:T(8,128)(2,1)S(1)}, u32[]{:S(2)}, u32[]{:S(2)}) collective-permute-start(bf16[224,512]{1,0:T(8,128)(2,1)} %get-tuple-element.73), channel_id=1, source_target_pairs={{0,112},{1,32},{2,80},{3,0},{4,48},{5,96},{6,16},{7,64},{8,120},{9... | collective-permute-start | bytes 688136 | tf_op jit(solution)/shard_map/ppermute | solution.py:331
  177.2 4.6 %collective-permute-start.33 = (bf16[224,512]{1,0:T(8,128)(2,1)}, bf16[224,512]{1,0:T(8,128)(2,1)}, u32[]{:S(2)}, u32[]{:S(2)}) collective-permute-start(bf16[224,512]{1,0:T(8,128)(2,1)} %get-tuple-element.74), channel_id=1, source_target_pairs={{0,120},{1,40},{2,88},{3,8},{4,56},{5,104},{6,24},{7,72},{8,96},{9... | collective-permute-start | bytes 688136 | tf_op jit(solution)/shard_map/ppermute | solution.py:331
  182.0 7.1 %fusion.refs_32_ = f32[1792,512]{1,0:T(8,128)S(1)} fusion(bf16[2048,1792]{1,0:T(8,128)(2,1)} %all-gather.3.cloned.1.call-done.acts, bf16[2048,512]{1,0:T(8,128)(2,1)} %all-gather.5.cloned.1.call-done), kind=kOutput, calls=%fused_computation | convolution fusion | flops 3758096384 | bytes 13107200 | tf_op jit(solution)/shard_map/dot_general | solution.py:338
  189.2 18.4 %update.1 = (f32[1792,512]{1,0:T(8,128)}, f32[1792,512]{1,0:T(8,128)}, f32[1792,512]{1,0:T(8,128)}) custom-call(bf16[112,512]{1,0:T(8,128)(2,1)S(1)} %collective-permute-done.2.refs_0_, bf16[112,512]{1,0:T(8,128)(2,1)S(1)} %copy-done.6, bf16[112,512]{1,0:T(8,128)(2,1)S(1)} %copy-done.8, bf16[112,512]{1,0:T(8,128)(2,1)S(1)} %copy-done.10, ...), custom_call_target="tpu_custom_call" | custom-call | flops 27525120 | bytes 20971520 | tf_op jit(solution)/shard_map/update/pallas_call | solution.py:297
  (140 shorter events, 56.3 us)
Async XLA Ops:
  7.2 90.4 %all-gather.3.cloned.1.call-start = ((), (), s32[]{:S(2)}) async-start(), calls=%async_computation.1 | async-start | bytes 7798784 | tf_op jit(solution)/shard_map/all_gather | solution.py:318
  7.9 173.9 %all-gather.5.cloned.1.call-start = ((), (), s32[]{:S(2)}) async-start(), calls=%async_computation.3 | async-start | bytes 2359296 | tf_op jit(solution)/shard_map/all_gather | solution.py:335
  8.6 199.1 %reduce-scatter.2.cloned.1.call-start = ((), (), s32[]{:S(2)}) async-start(), calls=%async_computation.2 | async-start | bytes 2359296 | tf_op jit(solution)/shard_map/reduce_scatter | solution.py:337
  31.8 21.2 %collective-permute-start.2 = (bf16[112,512]{1,0:T(8,128)(2,1)S(1)}, bf16[112,512]{1,0:T(8,128)(2,1)S(1)}, u32[]{:S(2)}, u32[]{:S(2)}) collective-permute-start(bf16[112,512]{1,0:T(8,128)(2,1)S(1)} %get-tuple-element.43), channel_id=1, source_target_pairs={{0,0},{1,80},{2,96},{3,48},{4,64},{5,16},{6,32},{7,112},{8,8},{9,8... | collective-permute-start | bytes 344072 | tf_op jit(solution)/shard_map/ppermute | solution.py:331
  42.9 19.2 %collective-permute-start.4 = (bf16[112,512]{1,0:T(8,128)(2,1)S(1)}, bf16[112,512]{1,0:T(8,128)(2,1)S(1)}, u32[]{:S(2)}, u32[]{:S(2)}) collective-permute-start(bf16[112,512]{1,0:T(8,128)(2,1)S(1)} %get-tuple-element.45), channel_id=1, source_target_pairs={{0,16},{1,64},{2,112},{3,32},{4,80},{5,0},{6,48},{7,96},{8,24},{9,... | collective-permute-start | bytes 344072 | tf_op jit(solution)/shard_map/ppermute | solution.py:331
  44.8 19.7 %collective-permute-start.5 = (bf16[112,512]{1,0:T(8,128)(2,1)S(1)}, bf16[112,512]{1,0:T(8,128)(2,1)S(1)}, u32[]{:S(2)}, u32[]{:S(2)}) collective-permute-start(bf16[112,512]{1,0:T(8,128)(2,1)S(1)} %get-tuple-element.46), channel_id=1, source_target_pairs={{0,24},{1,72},{2,120},{3,40},{4,88},{5,8},{6,56},{7,104},{8,0},{9,... | collective-permute-start | bytes 344072 | tf_op jit(solution)/shard_map/ppermute | solution.py:331
  48.5 17.9 %collective-permute-start.6 = (bf16[112,512]{1,0:T(8,128)(2,1)S(1)}, bf16[112,512]{1,0:T(8,128)(2,1)S(1)}, u32[]{:S(2)}, u32[]{:S(2)}) collective-permute-start(bf16[112,512]{1,0:T(8,128)(2,1)S(1)} %get-tuple-element.47), channel_id=1, source_target_pairs={{0,32},{1,112},{2,0},{3,80},{4,96},{5,48},{6,64},{7,16},{8,40},{9,... | collective-permute-start | bytes 344072 | tf_op jit(solution)/shard_map/ppermute | solution.py:331
  56.6 16.9 %collective-permute-start.8 = (bf16[112,512]{1,0:T(8,128)(2,1)S(1)}, bf16[112,512]{1,0:T(8,128)(2,1)S(1)}, u32[]{:S(2)}, u32[]{:S(2)}) collective-permute-start(bf16[112,512]{1,0:T(8,128)(2,1)S(1)} %get-tuple-element.49), channel_id=1, source_target_pairs={{0,48},{1,96},{2,16},{3,64},{4,112},{5,32},{6,80},{7,0},{8,56},{9,... | collective-permute-start | bytes 344072 | tf_op jit(solution)/shard_map/ppermute | solution.py:331
  62.1 16.3 %collective-permute-start.9 = (bf16[112,512]{1,0:T(8,128)(2,1)S(1)}, bf16[112,512]{1,0:T(8,128)(2,1)S(1)}, u32[]{:S(2)}, u32[]{:S(2)}) collective-permute-start(bf16[112,512]{1,0:T(8,128)(2,1)S(1)} %get-tuple-element.50), channel_id=1, source_target_pairs={{0,56},{1,104},{2,24},{3,72},{4,120},{5,40},{6,88},{7,8},{8,32},{9... | collective-permute-start | bytes 344072 | tf_op jit(solution)/shard_map/ppermute | solution.py:331
  64.5 17.1 %collective-permute-start.10 = (bf16[112,512]{1,0:T(8,128)(2,1)S(1)}, bf16[112,512]{1,0:T(8,128)(2,1)S(1)}, u32[]{:S(2)}, u32[]{:S(2)}) collective-permute-start(bf16[112,512]{1,0:T(8,128)(2,1)S(1)} %get-tuple-element.51), channel_id=1, source_target_pairs={{0,64},{1,16},{2,32},{3,112},{4,0},{5,80},{6,96},{7,48},{8,72},{9,... | collective-permute-start | bytes 344072 | tf_op jit(solution)/shard_map/ppermute | solution.py:331
  68.6 18.6 %collective-permute-start.12 = (bf16[112,512]{1,0:T(8,128)(2,1)S(1)}, bf16[112,512]{1,0:T(8,128)(2,1)S(1)}, u32[]{:S(2)}, u32[]{:S(2)}) collective-permute-start(bf16[112,512]{1,0:T(8,128)(2,1)S(1)} %get-tuple-element.53), channel_id=1, source_target_pairs={{0,80},{1,0},{2,48},{3,96},{4,16},{5,64},{6,112},{7,32},{8,88},{9,... | collective-permute-start | bytes 344072 | tf_op jit(solution)/shard_map/ppermute | solution.py:331
  73.6 18.9 %collective-permute-start.13 = (bf16[112,512]{1,0:T(8,128)(2,1)S(1)}, bf16[112,512]{1,0:T(8,128)(2,1)S(1)}, u32[]{:S(2)}, u32[]{:S(2)}) collective-permute-start(bf16[112,512]{1,0:T(8,128)(2,1)S(1)} %get-tuple-element.54), channel_id=1, source_target_pairs={{0,88},{1,8},{2,56},{3,104},{4,24},{5,72},{6,120},{7,40},{8,64},{9... | collective-permute-start | bytes 344072 | tf_op jit(solution)/shard_map/ppermute | solution.py:331
  121.7 19.9 %collective-permute-start.18 = (bf16[224,512]{1,0:T(8,128)(2,1)S(1)}, bf16[224,512]{1,0:T(8,128)(2,1)S(1)}, u32[]{:S(2)}, u32[]{:S(2)}) collective-permute-start(bf16[224,512]{1,0:T(8,128)(2,1)S(1)} %get-tuple-element.59), channel_id=1, source_target_pairs={{0,0},{1,80},{2,96},{3,48},{4,64},{5,16},{6,32},{7,112},{8,8},{9,8... | collective-permute-start | bytes 688136 | tf_op jit(solution)/shard_map/ppermute | solution.py:331
  128.8 16.4 %collective-permute-start.19 = (bf16[224,512]{1,0:T(8,128)(2,1)S(1)}, bf16[224,512]{1,0:T(8,128)(2,1)S(1)}, u32[]{:S(2)}, u32[]{:S(2)}) collective-permute-start(bf16[224,512]{1,0:T(8,128)(2,1)S(1)} %get-tuple-element.60), channel_id=1, source_target_pairs={{0,8},{1,88},{2,104},{3,56},{4,72},{5,24},{6,40},{7,120},{8,16},{9... | collective-permute-start | bytes 688136 | tf_op jit(solution)/shard_map/ppermute | solution.py:331
  130.7 21.6 %collective-permute-start.20 = (bf16[224,512]{1,0:T(8,128)(2,1)S(1)}, bf16[224,512]{1,0:T(8,128)(2,1)S(1)}, u32[]{:S(2)}, u32[]{:S(2)}) collective-permute-start(bf16[224,512]{1,0:T(8,128)(2,1)S(1)} %get-tuple-element.61), channel_id=1, source_target_pairs={{0,16},{1,64},{2,112},{3,32},{4,80},{5,0},{6,48},{7,96},{8,24},{9,... | collective-permute-start | bytes 688136 | tf_op jit(solution)/shard_map/ppermute | solution.py:331
  134.6 19.8 %collective-permute-start.21 = (bf16[224,512]{1,0:T(8,128)(2,1)S(1)}, bf16[224,512]{1,0:T(8,128)(2,1)S(1)}, u32[]{:S(2)}, u32[]{:S(2)}) collective-permute-start(bf16[224,512]{1,0:T(8,128)(2,1)S(1)} %get-tuple-element.62), channel_id=1, source_target_pairs={{0,24},{1,72},{2,120},{3,40},{4,88},{5,8},{6,56},{7,104},{8,0},{9,... | collective-permute-start | bytes 688136 | tf_op jit(solution)/shard_map/ppermute | solution.py:331
  135.7 20.6 %collective-permute-start.22 = (bf16[224,512]{1,0:T(8,128)(2,1)S(1)}, bf16[224,512]{1,0:T(8,128)(2,1)S(1)}, u32[]{:S(2)}, u32[]{:S(2)}) collective-permute-start(bf16[224,512]{1,0:T(8,128)(2,1)S(1)} %get-tuple-element.63), channel_id=1, source_target_pairs={{0,32},{1,112},{2,0},{3,80},{4,96},{5,48},{6,64},{7,16},{8,40},{9,... | collective-permute-start | bytes 688136 | tf_op jit(solution)/shard_map/ppermute | solution.py:331
  145.2 18.3 %collective-permute-start.24 = (bf16[224,512]{1,0:T(8,128)(2,1)S(1)}, bf16[224,512]{1,0:T(8,128)(2,1)S(1)}, u32[]{:S(2)}, u32[]{:S(2)}) collective-permute-start(bf16[224,512]{1,0:T(8,128)(2,1)S(1)} %get-tuple-element.65), channel_id=1, source_target_pairs={{0,48},{1,96},{2,16},{3,64},{4,112},{5,32},{6,80},{7,0},{8,56},{9,... | collective-permute-start | bytes 688136 | tf_op jit(solution)/shard_map/ppermute | solution.py:331
  152.3 18.6 %collective-permute-start.25 = (bf16[224,512]{1,0:T(8,128)(2,1)S(1)}, bf16[224,512]{1,0:T(8,128)(2,1)S(1)}, u32[]{:S(2)}, u32[]{:S(2)}) collective-permute-start(bf16[224,512]{1,0:T(8,128)(2,1)S(1)} %get-tuple-element.66), channel_id=1, source_target_pairs={{0,56},{1,104},{2,24},{3,72},{4,120},{5,40},{6,88},{7,8},{8,32},{9... | collective-permute-start | bytes 688136 | tf_op jit(solution)/shard_map/ppermute | solution.py:331
  154.4 18.4 %collective-permute-start.26 = (bf16[224,512]{1,0:T(8,128)(2,1)S(1)}, bf16[224,512]{1,0:T(8,128)(2,1)S(1)}, u32[]{:S(2)}, u32[]{:S(2)}) collective-permute-start(bf16[224,512]{1,0:T(8,128)(2,1)S(1)} %get-tuple-element.67), channel_id=1, source_target_pairs={{0,64},{1,16},{2,32},{3,112},{4,0},{5,80},{6,96},{7,48},{8,72},{9,... | collective-permute-start | bytes 688136 | tf_op jit(solution)/shard_map/ppermute | solution.py:331
  156.3 16.8 %collective-permute-start.27 = (bf16[224,512]{1,0:T(8,128)(2,1)S(1)}, bf16[224,512]{1,0:T(8,128)(2,1)S(1)}, u32[]{:S(2)}, u32[]{:S(2)}) collective-permute-start(bf16[224,512]{1,0:T(8,128)(2,1)S(1)} %get-tuple-element.68), channel_id=1, source_target_pairs={{0,72},{1,24},{2,40},{3,120},{4,8},{5,88},{6,104},{7,56},{8,80},{9... | collective-permute-start | bytes 688136 | tf_op jit(solution)/shard_map/ppermute | solution.py:331
  156.9 20.4 %collective-permute-start.28 = (bf16[224,512]{1,0:T(8,128)(2,1)S(1)}, bf16[224,512]{1,0:T(8,128)(2,1)S(1)}, u32[]{:S(2)}, u32[]{:S(2)}) collective-permute-start(bf16[224,512]{1,0:T(8,128)(2,1)S(1)} %get-tuple-element.69), channel_id=1, source_target_pairs={{0,80},{1,0},{2,48},{3,96},{4,16},{5,64},{6,112},{7,32},{8,88},{9,... | collective-permute-start | bytes 688136 | tf_op jit(solution)/shard_map/ppermute | solution.py:331
  163.5 25.5 %collective-permute-start.29 = (bf16[224,512]{1,0:T(8,128)(2,1)}, bf16[224,512]{1,0:T(8,128)(2,1)S(1)}, u32[]{:S(2)}, u32[]{:S(2)}) collective-permute-start(bf16[224,512]{1,0:T(8,128)(2,1)} %get-tuple-element.70), channel_id=1, source_target_pairs={{0,88},{1,8},{2,56},{3,104},{4,24},{5,72},{6,120},{7,40},{8,64},{9... | collective-permute-start | bytes 688136 | tf_op jit(solution)/shard_map/ppermute | solution.py:331
  170.9 18.1 %collective-permute-start.30 = (bf16[224,512]{1,0:T(8,128)(2,1)}, bf16[224,512]{1,0:T(8,128)(2,1)S(1)}, u32[]{:S(2)}, u32[]{:S(2)}) collective-permute-start(bf16[224,512]{1,0:T(8,128)(2,1)} %get-tuple-element.71), channel_id=1, source_target_pairs={{0,96},{1,48},{2,64},{3,16},{4,32},{5,112},{6,0},{7,80},{8,104},{9... | collective-permute-start | bytes 688136 | tf_op jit(solution)/shard_map/ppermute | solution.py:331
  (53 other events, 747.4 us)
Sparse Core Ops, SparseCore 0:
  10.2 87.2 all-gather.2
  99.2 25.5 all-gather.4
  127.8 56.6 reduce-scatter.1
